TPU v7x, 32 devices: a whole 2x2x4 slice. The times are simulated.
32 devices in a mesh: lat: 2 (over x), lon: 4 (over z), lev: 4 (over y, core).
Axes of the slice: x: 2, y: 2, z: 4, core: 2. Of those that a mesh axis runs over, the one named last changes fastest.
Arguments:
- fields: float32 [3, 16, 1280, 3072], P(None, 'lev', 'lat', 'lon'), may hold values from -6 to 6
- sl_weights: float32 [40, 24, 128, 128], P('lat', 'lon'), may hold values from -0.5 to 0.5
- sl_tile: int32 [40, 24], P('lat', 'lon'), may hold values from -1 to 1
- daylit: int32 [1280, 24], P('lat', 'lon'), may hold values from 0 to 1, as said below
- absorption: float32 [32], replicated, may hold values from 0.05 to 5
- continuum: float32 [32], replicated, may hold values from 0.05 to 2
- albedo: float32 [32], replicated, may hold values from 0.5 to 0.95
- wave_ids: int32 [640], replicated, may hold values from 0 to 639, each once
- legendre: float32 [640, 640, 1280], P(('lat', 'lon'), 'lev'), may hold values from -0.15625 to 0.15625
Outputs:
- spectral: float32 [640, 2, 3, 16, 640], P(('lat', 'lon'), None, None, None, 'lev')
Inputs may be any that keep to these rules, and one draw needn't show every extreme that they name: `daylit`: in every latitude row, at most one of the blocks b and b + 12 is sunlit. `wave_ids`: every wavenumber appears in exactly one slot.
All inputs are finite; a program needn't handle non-finite values.
Results may differ from a plain program's by a relative error of at most 0.000068.
Values sent between devices are 32-bit elements; how exact they have to be, the bound alone decides.
A program may use at most 320 MiB of HBM per device.

v0:
```python
import math

import jax
import jax.numpy as jnp
from jax import lax
from jax.sharding import PartitionSpec as P

highest = lax.Precision.HIGHEST
heat_rate = 6.0
asymmetry = 0.6


def with_halo(block, sides, width):
    for axis, dim in sides:
        count = lax.axis_size(axis)
        forward = [(i, i + 1) for i in range(count - 1)]
        forward.append((count - 1, 0))
        backward = [(target, source) for source, target in forward]
        low = lax.ppermute(
            lax.slice_in_dim(block, block.shape[dim] - width, None, axis=dim), axis, forward
        )
        high = lax.ppermute(lax.slice_in_dim(block, 0, width, axis=dim), axis, backward)
        block = jnp.concatenate([low, block, high], axis=dim)
    return block


def carried_in(value, axis, join, neutral):
    count, mine = (lax.axis_size(axis), lax.axis_index(axis))
    pieces = jax.tree.map(lambda part: lax.all_gather(part, axis), value)
    subtotal = jax.tree.map(
        lambda part, zero: jnp.full_like(part, 0) + jnp.asarray(zero, part.dtype), value, neutral
    )

    def turn(position, subtotal):
        longer = join(subtotal, jax.tree.map(lambda part: part[position], pieces))
        return jax.tree.map(lambda new, old: jnp.where(position < mine, new, old), longer, subtotal)

    return lax.fori_loop(0, count - 1, turn, subtotal)


def absorbed_per_band(
    depth_wet,
    hot_extinction_thickness,
    above_wet,
    above_warm,
    absorb_part,
    continuum_part,
    reflectivity_share,
):
    gamma_one = (7.0 - reflectivity_share * (4.0 + 3.0 * asymmetry)) / 4.0
    gamma_two = -(1.0 - reflectivity_share * (4.0 - 3.0 * asymmetry)) / 4.0
    eigen_rate = jnp.sqrt(gamma_one * gamma_one - gamma_two * gamma_two)
    optical = absorb_part * depth_wet + continuum_part * hot_extinction_thickness
    beam = jnp.exp(-(absorb_part * above_wet + continuum_part * above_warm))
    decay = jnp.exp(-eigen_rate * optical)
    decay_sq = decay * decay
    denominator = eigen_rate + gamma_one + (eigen_rate - gamma_one) * decay_sq
    reflect = gamma_two * (1.0 - decay_sq) / denominator
    transmit = 2.0 * eigen_rate * decay / denominator
    return beam * (1.0 - reflect - transmit)


def absorbed_mean(
    depth_wet, hot_extinction_thickness, above_wet, above_warm, absorption, continuum, albedo
):
    band_total = absorption.shape[0]
    band_group = min(8, band_total)
    unit_shape = (1,) * depth_wet.ndim
    running = jnp.zeros_like(depth_wet)
    for band_start in range(0, band_total, band_group):
        absorb_part = absorption[band_start : band_start + band_group].reshape(
            (band_group,) + unit_shape
        )
        continuum_part = continuum[band_start : band_start + band_group].reshape(
            (band_group,) + unit_shape
        )
        reflectivity_share = albedo[band_start : band_start + band_group].reshape(
            (band_group,) + unit_shape
        )
        terms = absorbed_per_band(
            depth_wet[None],
            hot_extinction_thickness[None],
            above_wet[None],
            above_warm[None],
            absorb_part,
            continuum_part,
            reflectivity_share,
        )
        running = running + jnp.sum(terms, axis=0)
    return running / band_total


def add_pair(earlier, later):
    return (earlier[0] + later[0], earlier[1] + later[1])


def local(fields, sl_weights, sl_tile, daylit, absorption, continuum, albedo, wave_ids, legendre):
    meridian_number = lax.axis_size("lon")
    lat_count = lax.axis_size("lat")
    lev_count = lax.axis_size("lev")
    wave_devices = lat_count * meridian_number
    field_count, lev_local, lat_local, lon_local = fields.shape
    tile_width = sl_weights.shape[-1]
    tile_count = lon_local // tile_width
    row_blocks = sl_tile.shape[0]
    block_rows = lat_local // row_blocks
    padded = with_halo(fields, (("lon", 3),), tile_width)
    tile_rows = padded.reshape(
        field_count, lev_local, row_blocks, block_rows, tile_count + 2, tile_width
    )
    source_ids = jnp.arange(tile_count, dtype=jnp.int32)[None, :] + 1 + sl_tile
    onehot = (
        source_ids[:, :, None] == jnp.arange(tile_count + 2, dtype=jnp.int32)[None, None, :]
    ).astype(jnp.float32)
    sources = jnp.einsum("flbrkc,bjk->flbrjc", tile_rows, onehot, precision=highest)
    departure_estimate = jnp.einsum("flbrjc,bjtc->flbrjt", sources, sl_weights, precision=highest)
    departure_estimate = departure_estimate.reshape(field_count, lev_local, lat_local, lon_local)
    moisture = departure_estimate[2]
    thermal_state = departure_estimate[0]
    stratum_factor = 4.0 / (lev_local * lev_count)
    depth_wet = stratum_factor * (0.2 + moisture * moisture)
    hot_extinction_thickness = stratum_factor * (0.2 + thermal_state * thermal_state)
    zeros_plane = jnp.zeros((lat_local, lon_local), jnp.float32)
    prefix_wet, prefix_warm = carried_in(
        (jnp.sum(depth_wet, axis=0), jnp.sum(hot_extinction_thickness, axis=0)),
        "lev",
        add_pair,
        (zeros_plane, zeros_plane),
    )
    wet_levels = []
    warm_levels = []
    for level in range(lev_local):
        wet_levels.append(prefix_wet)
        warm_levels.append(prefix_warm)
        prefix_wet = prefix_wet + depth_wet[level]
        prefix_warm = prefix_warm + hot_extinction_thickness[level]
    above_wet = jnp.stack(wet_levels, axis=0)
    above_warm = jnp.stack(warm_levels, axis=0)
    absorbed = absorbed_mean(
        depth_wet, hot_extinction_thickness, above_wet, above_warm, absorption, continuum, albedo
    )
    absorbed = absorbed.reshape(lev_local, lat_local, tile_count, tile_width)
    heating = (absorbed * daylit.astype(jnp.float32)[None, :, :, None]).reshape(
        lev_local, lat_local, lon_local
    )
    updated = jnp.concatenate(
        [departure_estimate[:1] + heat_rate * heating[None], departure_estimate[1:]], axis=0
    )
    rows_each = lat_local // meridian_number
    mesh_lines = updated.reshape(field_count, lev_local, meridian_number, rows_each, lon_local)
    whole_rows = lax.all_to_all(mesh_lines, "lon", split_axis=2, concat_axis=4, tiled=True)
    whole_rows = whole_rows.reshape(field_count, lev_local, rows_each, lon_local * meridian_number)
    lon_total = whole_rows.shape[-1]
    wave_total = wave_ids.shape[0]
    phases = wave_ids[:, None] * jnp.arange(lon_total, dtype=jnp.int32)[None, :] % lon_total
    angles = phases.astype(jnp.float32) * (2.0 * math.pi / lon_total)
    dft_table = (
        jnp.stack([jnp.cos(angles), -jnp.sin(angles)], axis=1) / math.sqrt(lon_total)
    ).reshape(2 * wave_total, lon_total)
    fourier = jnp.einsum("wn,flrn->wflr", dft_table, whole_rows, precision=highest)
    waves_local = wave_total // wave_devices
    outgoing_waves = fourier.reshape(
        wave_devices, 2 * waves_local, field_count, lev_local, 1, rows_each
    )
    arrived = lax.all_to_all(
        outgoing_waves, ("lat", "lon"), split_axis=0, concat_axis=4, tiled=True
    )
    spectral_in = arrived.reshape(waves_local, 2, field_count, lev_local, wave_devices * rows_each)
    spectra = jnp.einsum(
        "mcfls,mns->mcfln",
        lax.all_gather(spectral_in, "lev", axis=3, tiled=True),
        legendre,
        precision=highest,
    )
    degree_local = legendre.shape[1]
    degrees = lax.axis_index("lev") * degree_local + jnp.arange(degree_local, dtype=jnp.int32)
    own_waves = lax.dynamic_slice_in_dim(
        wave_ids, lax.axis_index(("lat", "lon")) * waves_local, waves_local
    )
    keep_mask = degrees[None, :] >= own_waves[:, None]
    return jnp.where(keep_mask[:, None, None, None, :], spectra, 0.0)


def solution(mesh):
    in_specs = (
        P(None, "lev", "lat", "lon"),
        P("lat", "lon", None, None),
        P("lat", "lon"),
        P("lat", "lon"),
        P(),
        P(),
        P(),
        P(),
        P(("lat", "lon"), "lev", None),
    )
    out_specs = P(("lat", "lon"), None, None, None, "lev")
    return jax.shard_map(local, mesh=mesh, in_specs=in_specs, out_specs=out_specs, check_vma=False)
```

profile of v0, /device:TPU:0, one launch (start us, length us, event | category | flops | bytes accessed | tf_op | source)
XLA Modules:
  0.0 2256.8 jit_solution(4369819479675837928)
XLA Ops:
  6.5 7.2 fusion.52
  13.8 5.0 collective-permute-start.1
  19.0 85.5 %collective-permute-done.1 = f32[3,4,640,128]{3,2,1,0:T(8,128)} collective-permute-done((f32[3,4,640,128]{3,2,1,0:T(8,128)}, f32[3,4,640,128]{3,2,1,0:T(8,128)}, u32[]{:S(2)}, u32[]{:S(2)}) %collective-permute-start.1) | collective-permute-done | bytes 3932192 | tf_op jit(solution)/shard_map/ppermute | solution.py:22
  104.5 84.0 %collective-permute-done = f32[3,4,640,128]{3,2,1,0:T(8,128)} collective-permute-done((f32[3,4,640,128]{3,2,1,0:T(8,128)}, f32[3,4,640,128]{3,2,1,0:T(8,128)}, u32[]{:S(2)}, u32[]{:S(2)}) %collective-permute-start) | collective-permute-done | bytes 3932192 | tf_op jit(solution)/shard_map/ppermute | solution.py:19
  188.5 11.9 pad_maximum_fusion
  200.4 14.0 copy.140
  214.4 29.2 %fusion.9 = f32[3,4,20,32,6,128]{5,4,3,1,0,2:T(8,128)} fusion(f32[3,4,20,32,8,128]{5,4,3,2,1,0:T(8,128)} %bitcast.107, s32[20,6]{1,0:T(8,128)S(1)} %copy.114), kind=kOutput, calls=%fused_computation.18 | convolution fusion | flops 566232000 | bytes 55050720 | tf_op jit(solution)/shard_map/flbrkc,bjk->flbrjc/dot_general | solution.py:115
  243.6 31.5 %fusion.12 = f32[3,4,20,32,6,128]{5,3,1,0,4,2:T(8,128)} fusion(f32[3,4,20,32,6,128]{5,4,3,1,0,2:T(8,128)} %fusion.9, f32[20,6,128,128]{3,2,1,0:T(8,128)} %param.12), kind=kOutput, calls=%fused_computation.20 | convolution fusion | flops 9059696640 | bytes 55050240 | tf_op jit(solution)/shard_map/flbrjc,bjtc->flbrjt/dot_general | solution.py:116
  275.1 14.5 fusion.46
  303.8 14.9 slice.113
  318.8 20.1 copy.129
  338.9 20.7 concatenate.10
  359.6 15.4 copy.117
  374.9 11.3 slice.84
  386.3 14.9 copy.127
  401.2 11.0 mul.557
  412.3 14.9 copy.126
  427.1 11.1 mul.554
  438.2 8.1 fusion.53
  446.3 4.7 copy.125
  451.0 4.6 copy.124
  467.7 15.0 while.16
  467.9 4.5 add_select_fusion.4
  472.4 5.1 add_select_fusion.4
  477.5 5.1 add_select_fusion.4
  482.6 5.6 fusion.31
  488.3 4.3 pad_maximum_fusion.3
  499.5 120.2 %multiply_reduce_fusion.3 = (f32[4,640,768]{2,1,0:T(8,128)}, f32[4,640,768]{2,1,0:T(8,128)}) fusion(f32[8]{0:T(128)S(1)} %get-tuple-element.210, f32[8]{0:T(128)S(1)} %get-tuple-element.208, f32[8]{0:T(128)S(1)} %get-tuple-element.209, f32[4,640,768]{2,1,0:T(8,128)} %mul.557, f32[4,640,768]{2,1,0:T(8,128)} %mul.554, f32[8]{0:T(128)S(1)} %get-tuple-element.215, ...), kind=kLoop, calls=%fused_computation.7 | loop fusion | flops 625213440 | bytes 47186368 | tf_op jit(solution)/shard_map/reduce_sum | solution.py:89
  619.7 120.1 %multiply_reduce_fusion.2 = (f32[4,640,768]{2,1,0:T(8,128)}, f32[4,640,768]{2,1,0:T(8,128)}) fusion(f32[8]{0:T(128)S(1)} %get-tuple-element.207, f32[8]{0:T(128)S(1)} %get-tuple-element.205, f32[8]{0:T(128)S(1)} %get-tuple-element.206, f32[8]{0:T(128)S(1)} %get-tuple-element.218, f32[8]{0:T(128)S(1)} %get-tuple-element.220, f32[8]{0:T(128)S(1)} %get-tuple-element.202, ...), kind=kLoop, calls=%fused_computation.6 | loop fusion | flops 625213440 | bytes 47186368 | tf_op jit(solution)/shard_map/reduce_sum | solution.py:89
  739.8 14.5 add_add_fusion
  754.3 9.9 multiply_add_fusion
  764.2 9.4 pad_maximum_fusion.1
  773.6 8.2 copy.130
  781.8 8.3 all-to-all-start
  790.2 34.9 %fusion.25 = (f32[640,1,3072]{2,0,1:T(8,128)}, f32[640,1,3072]{2,0,1:T(8,128)}) fusion(s32[640]{0:T(1024)S(1)} %copy-done.10), kind=kLoop, calls=%fused_computation.37 | loop fusion | flops 19660800 | bytes 15731200 | tf_op jit(solution)/shard_map/cos | solution.py:158
  825.1 14.4 maximum_multiply_fusion
  839.5 27.1 %copy.113 = f32[640,2,3072]{2,1,0:T(2,128)} copy(f32[640,2,3072]{2,0,1:T(8,128)} %maximum_multiply_fusion) | data formatting | bytes 31457280 | tf_op jit(solution)/shard_map/div | solution.py:158
  866.6 19.4 reshape.373
  885.9 413.5 %all-to-all-done = f32[3,4,4,160,768]{4,3,1,0,2:T(8,128)} async-done(((f32[3,4,4,160,768]{4,3,1,0,2:T(8,128)}), f32[3,4,4,160,768]{4,3,1,0,2:T(8,128)}, u32[]{:S(2)}, u32[]{:S(2)}) %all-to-all-start) | async-done | bytes 23592992 | tf_op jit(solution)/shard_map/all_to_all | solution.py:151
  1299.4 28.6 %copy.131 = f32[3,4,1,160,4,768]{5,4,3,1,0,2:T(4,128)} copy(f32[3,4,1,160,4,768]{5,3,1,0,4,2:T(8,128)} %bitcast.17) | data formatting | bytes 47185920 | tf_op jit(solution)/shard_map/all_to_all | solution.py:151
  1328.0 28.4 %reshape.374 = f32[3,4,160,3072,1]{3,2,1,0,4:T(8,128)} reshape(f32[3,4,1,160,4,768]{5,4,3,1,0,2:T(4,128)} %copy.131) | data formatting | bytes 47185920 | tf_op jit(solution)/shard_map/reshape.185
  1356.4 163.0 %fusion.15 = f32[8,160,3,4,1,160]{5,1,3,2,4,0:T(8,128)} fusion(f32[3,4,160,3072,1]{3,2,1,0,4:T(8,128)} %reshape.374, f32[8,160,3072,1,1]{2,1,0,3,4:T(8,128)} %reshape.373), kind=kOutput, calls=%fused_computation.21 | convolution fusion | flops 90596966400 | bytes 49152000 | tf_op jit(solution)/shard_map/wn,flrn->wflr/dot_general | solution.py:160
  1519.4 349.1 %all_to_all.30 = f32[8,160,3,4,1,160]{5,1,3,2,4,0:T(8,128)} all-to-all(f32[8,160,3,4,1,160]{5,1,3,2,4,0:T(8,128)} %fusion.15), channel_id=1, replica_groups=mesh['lat'=2,'lon'=4,'lev'=4] {'lat','lon'}, dimensions={0} | all-to-all | bytes 19660800 | tf_op jit(solution)/shard_map/all_to_all | solution.py:165
  1868.5 20.1 copy.133
  1888.6 16.9 reshape.370
  1905.5 10.7 copy.134
  1916.4 233.4 %all-gather.8.cloned.1.call-done = f32[80,2,3,16,1280]{4,0,2,1,3:T(8,128)} async-done(((f32[80,2,3,4,1280]{4,0,2,1,3:T(8,128)}), f32[80,2,3,16,1280]{4,0,2,1,3:T(8,128)}) %all-gather.8.cloned.1.call-update) | async-done | bytes 39321616 | tf_op jit(solution)/shard_map/all_gather | solution.py:171
  2149.8 100.2 %broadcast_select_fusion = f32[80,2,3,16,160]{4,3,2,1,0:T(8,128)} fusion(pred[80,160]{1,0:T(8,128)(4,1)S(1)} %broadcast_compare_fusion, f32[80,160,1280]{2,1,0:T(8,128)} %param.19, f32[80,2,3,16,1280]{4,0,2,1,3:T(8,128)} %all-gather.8.cloned.1.call-done), kind=kOutput, calls=%fused_computation.39 | convolution fusion | flops 18875596800 | bytes 109785600 | tf_op jit(solution)/shard_map/mcfls,mns->mcfln/dot_general | solution.py:169
  (59 shorter events, 33.4 us)
Async XLA Ops:
  6.5 12.3 copy-start.11
  6.5 461.1 %all-gather.4.cloned.1.call-start = ((), (), s32[]{:S(2)}) async-start(), calls=%async_computation.2 | async-start | bytes 9830400 | tf_op jit(solution)/shard_map/all_gather | solution.py:29
  13.8 90.7 %collective-permute-start.1 = (f32[3,4,640,128]{3,2,1,0:T(8,128)}, f32[3,4,640,128]{3,2,1,0:T(8,128)}, u32[]{:S(2)}, u32[]{:S(2)}) collective-permute-start(f32[3,4,640,128]{3,2,1,0:T(8,128)} %get-tuple-element.178), channel_id=1, source_target_pairs={{4,0},{8,4},{12,8},{0,12},{5,1},{9,5},{13,9},{1,13},{6,2},{10,6},{... | collective-permute-start | bytes 11796488 | tf_op jit(solution)/shard_map/ppermute | solution.py:22
  18.8 169.7 %collective-permute-start = (f32[3,4,640,128]{3,2,1,0:T(8,128)}, f32[3,4,640,128]{3,2,1,0:T(8,128)}, u32[]{:S(2)}, u32[]{:S(2)}) collective-permute-start(f32[3,4,640,128]{3,2,1,0:T(8,128)} %get-tuple-element.177), channel_id=1, source_target_pairs={{0,4},{4,8},{8,12},{12,0},{1,5},{5,9},{9,13},{13,1},{2,6},{6,10},{... | collective-permute-start | bytes 11796488 | tf_op jit(solution)/shard_map/ppermute | solution.py:19
  291.2 6.6 copy-start.7
  292.8 174.9 %all-gather.6.cloned.1.call-start = ((), (), s32[]{:S(2)}) async-start(), calls=%async_computation.3 | async-start | bytes 9830400 | tf_op jit(solution)/shard_map/all_gather | solution.py:29
  296.0 7.5 copy-start.9
  296.0 7.6 copy-start.6
  296.0 7.7 copy-start.8
  446.3 9.3 copy-start.5
  482.6 5.6 copy-start
  488.3 4.4 copy-start.1
  488.3 5.4 copy-start.2
  488.3 6.1 copy-start.3
  739.8 14.5 copy-start.4
  781.8 8.3 copy-start.10
  781.8 517.6 %all-to-all-start = ((f32[3,4,4,160,768]{4,3,1,0,2:T(8,128)}), f32[3,4,4,160,768]{4,3,1,0,2:T(8,128)}, u32[]{:S(2)}, u32[]{:S(2)}) async-start(f32[3,4,4,160,768]{4,3,1,0,2:T(8,128)} %copy.130), calls=%async_computation | async-start | bytes 47185920 | tf_op jit(solution)/shard_map/all_to_all | solution.py:151
  790.1 1359.7 %all-gather.8.cloned.1.call-start = ((), (), s32[]{:S(2)}) async-start(), calls=%async_computation.4 | async-start | bytes 49152000 | tf_op jit(solution)/shard_map/all_gather | solution.py:171
Sparse Core Ops, SparseCore 0:
  292.9 54.6 all-gather.3
  349.2 55.3 all-gather.5
  1916.3 233.4 all-gather.7
where the time goes:
time: 2270 us; the launch traced here: 2260 us
  waiting for transfers between devices  816 us (36%)
  other arithmetic  380 us (17%)
  local copies, waits for them, and re-layouts  360 us (16%)
  blocking collectives  349 us (15%)
  matrix products  324 us (14%)
    all_to_all x1, waiting for transfers between devices, local(): lax.all_to_all(mesh_lines, 'lon', split_axis=2, concat_axis=4, tiled=True)  414 us
    all_to_all x1, blocking collectives, local(): lax.all_to_all(outgoing_waves, ('lat', 'lon'), split_axis=0, concat_axis=...  349 us
    reduce_sum x2, other arithmetic, absorbed_mean(): running = running + jnp.sum(terms, axis=0)  240 us
    all_gather x1, waiting for transfers between devices, local(): lax.all_gather(spectral_in, 'lev', axis=3, tiled=True)  233 us
    dot_general x1, matrix products, local(): jnp.einsum('wn,flrn->wflr', dft_table, whole_rows, precision=highest)  163 us
    dot_general x1, matrix products, local(): jnp.einsum('mcfls,mns->mcfln', lax.all_gather(spectral_in, 'lev', axis=3,...  100 us
    ppermute x1, waiting for transfers between devices, with_halo(): lax.ppermute(lax.slice_in_dim(block, 0, width, axis=dim), axis, backward)  85.5 us
    ppermute x1, waiting for transfers between devices, with_halo(): lax.ppermute(lax.slice_in_dim(block, block.shape[dim] - width, None, axis...  84 us
  transfers between devices with their start and end apart: 6, of which 4 were waited for; matrix products, arithmetic and copies ran while one was open for 12% of the time, Pallas kernels for 0%

commit v1 on v0

v1 whole, which is shorter than its diff:
```python
import functools
import math

import jax
import jax.numpy as jnp
from jax import lax
from jax.experimental import pallas as pl
from jax.experimental.pallas import tpu as pltpu
from jax.sharding import PartitionSpec as P

high = lax.Precision.HIGH
heat_rate = 6.0
asymmetry = 0.6


def absorbed_kernel(bands, coef, dw_ref, dm_ref, aw_ref, am_ref, out_ref):
    def rows8(i, carry):
        rows = pl.ds(pl.multiple_of(i * 8, 8), 8)
        dw, dm, aw, am = dw_ref[rows, :], dm_ref[rows, :], aw_ref[rows, :], am_ref[rows, :]
        total = jnp.zeros_like(dw)
        for g in range(bands):
            beam = jnp.exp(coef[0, g] * aw + coef[1, g] * am)
            e = jnp.exp(coef[2, g] * dw + coef[3, g] * dm)
            e2 = e * e
            denominator = coef[4, g] + coef[5, g] * e2
            numerator = coef[6, g] + coef[7, g] * e2 - coef[8, g] * e
            total = total + beam * (numerator / denominator)
        out_ref[rows, :] = total * (1.0 / bands)
        return carry

    lax.fori_loop(0, out_ref.shape[0] // 8, rows8, 0)


def absorbed_mean(depth_wet, depth_warm, above_wet, above_warm, absorption, continuum, albedo):
    g1 = (7.0 - albedo * (4.0 + 3.0 * asymmetry)) / 4.0
    g2 = -(1.0 - albedo * (4.0 - 3.0 * asymmetry)) / 4.0
    k = jnp.sqrt(g1 * g1 - g2 * g2)
    coef = jnp.stack(
        [-absorption, -continuum, -k * absorption, -k * continuum, k + g1, k - g1,
         k + g1 - g2, k - g1 + g2, 2.0 * k]
    )
    shape = depth_wet.shape
    width = shape[-1]
    count = depth_wet.size // width
    block = math.gcd(count, 64)
    flat = [x.reshape(count, width) for x in (depth_wet, depth_warm, above_wet, above_warm)]
    spec = pl.BlockSpec((block, width), lambda i: (i, 0))
    bands = absorption.shape[0]
    out = pl.pallas_call(
        functools.partial(absorbed_kernel, bands),
        grid=(count // block,),
        in_specs=[pl.BlockSpec(memory_space=pltpu.SMEM)] + [spec] * 4,
        out_specs=spec,
        out_shape=jax.ShapeDtypeStruct((count, width), jnp.float32),
        cost_estimate=pl.CostEstimate(
            flops=20 * bands * count * width, bytes_accessed=20 * count * width,
            transcendentals=3 * bands * count * width,
        ),
    )(coef, *flat)
    return out.reshape(shape)


def local(fields, sl_weights, sl_tile, daylit, absorption, continuum, albedo, wave_ids, legendre):
    lon_n = lax.axis_size("lon")
    lat_n = lax.axis_size("lat")
    lev_n = lax.axis_size("lev")
    field_n, lev_l, lat_l, lon_l = fields.shape
    width = sl_weights.shape[-1]
    tiles = lon_l // width
    blocks = sl_tile.shape[0]
    block_rows = lat_l // blocks
    rows_each = lat_l // lon_n
    half = lon_n // 2
    forward = [(i, (i + 1) % lon_n) for i in range(lon_n)]
    backward = [(t, s) for s, t in forward]
    offset = sl_tile[None, :, None, :, None]

    def whole_rows(field):
        block = fields[field]
        low = lax.ppermute(block[:, :, lon_l - width :], "lon", forward)
        high_side = lax.ppermute(block[:, :, :width], "lon", backward)
        shape = (lev_l, blocks, block_rows, tiles, width)
        left = jnp.concatenate([low, block[:, :, : lon_l - width]], axis=2).reshape(shape)
        right = jnp.concatenate([block[:, :, width:], high_side], axis=2).reshape(shape)
        sources = jnp.where(offset < 0, left, jnp.where(offset > 0, right, block.reshape(shape)))
        interp = jnp.einsum("lbrjc,bjtc->lbrjt", sources, sl_weights, precision=high)
        lines = interp.reshape(lev_l, lon_n, rows_each, lon_l).transpose(1, 0, 2, 3)
        return lax.all_to_all(lines, "lon", split_axis=0, concat_axis=0, tiled=True)

    moisture = whole_rows(2)
    thermal = whole_rows(0)
    middle = whole_rows(1)

    sun = daylit.astype(jnp.float32).reshape(lon_n, rows_each, tiles)
    sun = lax.all_to_all(sun, "lon", split_axis=0, concat_axis=0, tiled=True)
    sun = jnp.broadcast_to(sun[..., None], (lon_n, rows_each, tiles, width))
    sun = sun.reshape(lon_n, 1, rows_each, lon_l)
    sun_near, sun_far = sun[:half], sun[half:]
    factor = 4.0 / (lev_l * lev_n)

    def depth_of(state):
        lit = jnp.where(sun_near > 0.0, state[:half], state[half:])
        return factor * (0.2 + lit * lit)

    depth_wet, depth_warm = depth_of(moisture), depth_of(thermal)
    totals = jnp.stack([jnp.sum(depth_wet, axis=1), jnp.sum(depth_warm, axis=1)])
    pieces = lax.all_gather(totals, "lev")
    mine = lax.axis_index("lev")
    prefix = jnp.zeros_like(totals)
    for group in range(lev_n - 1):
        prefix = prefix + jnp.where(group < mine, pieces[group], 0.0)

    def above_of(start, depth):
        levels = []
        for level in range(lev_l):
            levels.append(start)
            start = start + depth[:, level]
        return jnp.stack(levels, axis=1)

    absorbed = absorbed_mean(
        depth_wet, depth_warm, above_of(prefix[0], depth_wet), above_of(prefix[1], depth_warm),
        absorption, continuum, albedo,
    )
    heated = thermal + heat_rate * jnp.concatenate([absorbed * sun_near, absorbed * sun_far])

    lon_total = lon_l * lon_n
    wave_total = wave_ids.shape[0]
    phases = wave_ids[:, None] * jnp.arange(lon_total, dtype=jnp.int32)[None, :] % lon_total
    angles = phases.astype(jnp.float32) * (2.0 * math.pi / lon_total)
    table = jnp.stack([jnp.cos(angles), -jnp.sin(angles)], axis=1) / math.sqrt(lon_total)
    table = table.reshape(2 * wave_total, lon_total)
    waves_l = wave_total // (lat_n * lon_n)
    degree_l = legendre.shape[1]

    def spectra_of(state):
        lines = state.transpose(1, 2, 0, 3).reshape(lev_l * rows_each, lon_total)
        fourier = jnp.einsum("wn,xn->wx", table, lines, precision=high)
        out = fourier.reshape(lat_n, lon_n, 2 * waves_l, lev_l * rows_each)
        out = lax.all_to_all(out, "lat", split_axis=0, concat_axis=0, tiled=True)
        out = lax.all_to_all(out, "lon", split_axis=1, concat_axis=1, tiled=True)
        out = out.reshape(lat_n * lon_n, waves_l, 2 * lev_l, rows_each)
        out = out.transpose(1, 2, 0, 3).reshape(waves_l, 2 * lev_l, lat_n * lat_l)
        out = lax.all_gather(out, "lev")
        return jnp.einsum("Lmxs,mns->mLxn", out, legendre, precision=high)

    parts = [spectra_of(state) for state in (middle, moisture, heated)]
    spectra = jnp.stack([parts[2], parts[0], parts[1]], axis=1)
    spectra = spectra.reshape(waves_l, field_n, lev_n, 2, lev_l, degree_l)
    spectra = spectra.transpose(0, 3, 1, 2, 4, 5)
    spectra = spectra.reshape(waves_l, 2, field_n, lev_n * lev_l, degree_l)
    degrees = lax.axis_index("lev") * degree_l + jnp.arange(degree_l, dtype=jnp.int32)
    own_waves = lax.dynamic_slice_in_dim(
        wave_ids, lax.axis_index(("lat", "lon")) * waves_l, waves_l
    )
    keep_mask = degrees[None, :] >= own_waves[:, None]
    return jnp.where(keep_mask[:, None, None, None, :], spectra, 0.0)


def solution(mesh):
    in_specs = (
        P(None, "lev", "lat", "lon"),
        P("lat", "lon", None, None),
        P("lat", "lon"),
        P("lat", "lon"),
        P(),
        P(),
        P(),
        P(),
        P(("lat", "lon"), "lev", None),
    )
    out_specs = P(("lat", "lon"), None, None, None, "lev")
    return jax.shard_map(local, mesh=mesh, in_specs=in_specs, out_specs=out_specs, check_vma=False)
```

time: 2270 us -> 1760 us (0.78)
  waiting for transfers between devices: 816 us -> 451 us
  other arithmetic: 380 us -> 175 us
  local copies, waits for them, and re-layouts: 360 us -> 458 us
  Pallas kernels: 0 us -> 97.3 us
  matrix products: 324 us -> 235 us
  blocking collectives: 349 us -> 268 us
  starting transfers between devices: 13.4 us -> 49.7 us
    reduce_sum x3 -> x2, other arithmetic: 255 us -> 8.94 us  [the longest x1 6.11 us: local(): jnp.sum(depth_warm, axis=1)]
    all_gather x3 -> x4, waiting for transfers between devices: 233 us -> 4.26 us  [the longest x3 4.26 us: spectra_of(): out = lax.all_gather(out, 'lev')]
    ppermute x2 -> x6, waiting for transfers between devices: 170 us -> 0.02 us  [the longest x3 0.01 us: whole_rows(): low = lax.ppermute(block[:, :, lon_l - width:], 'lon', forward)]
    transpose x0 -> x13, local copies, waits for them, and re-layouts: none -> 127 us  [the longest x3 45.3 us: whole_rows(): jnp.einsum('lbrjc,bjtc->lbrjt', sources, sl_weights, precision=high)]
    reshape x2 -> x18, local copies, waits for them, and re-layouts: 27.6 us -> 148 us  [the longest x3 32.5 us: whole_rows(): lines = interp.reshape(lev_l, lon_n, rows_each, lon_l).transpose(1, 0, 2, 3)]
    pallas_call x0 -> x1, Pallas kernels: none -> 97.3 us  [absorbed_mean(): pl.pallas_call(functools.partial(absorbed_kernel, bands), grid=(count //...]
    dot_general x4 -> x9, matrix products: 324 us -> 235 us  [the longest x3 111 us: spectra_of(): return jnp.einsum('Lmxs,mns->mLxn', out, legendre, precision=high)]
    all_to_all x1 -> x5, blocking collectives: 349 us -> 268 us  [the longest x2 149 us: spectra_of(): out = lax.all_to_all(out, 'lon', split_axis=1, concat_axis=1, tiled=True)]
  transfers between devices with their start and end apart: 6 -> 15, of which waited for: 4 -> 5; matrix products, arithmetic and copies ran while one was open for 12% -> 44% of each run, Pallas kernels for 0% -> 6%
where the time goes in v1:
time: 1760 us; the launch traced here: 1750 us
  local copies, waits for them, and re-layouts  458 us (26%)
  waiting for transfers between devices  451 us (26%)
  blocking collectives  268 us (15%)
  matrix products  235 us (13%)
  other arithmetic  175 us (10%)
  Pallas kernels  97.3 us (6%)
  starting transfers between devices  49.7 us (3%)
    all_to_all x3, waiting for transfers between devices, whole_rows(): return lax.all_to_all(lines, 'lon', split_axis=0, concat_axis=0, tiled=True)  426 us
    all_to_all x2, blocking collectives, spectra_of(): out = lax.all_to_all(out, 'lon', split_axis=1, concat_axis=1, tiled=True)  149 us
    all_to_all x3, blocking collectives, spectra_of(): out = lax.all_to_all(out, 'lat', split_axis=0, concat_axis=0, tiled=True)  118 us
    dot_general x3, matrix products, spectra_of(): return jnp.einsum('Lmxs,mns->mLxn', out, legendre, precision=high)  111 us
    pallas_call x1, Pallas kernels, absorbed_mean(): pl.pallas_call(functools.partial(absorbed_kernel, bands), grid=(count //...  97.3 us
    dot_general x3, matrix products, spectra_of(): fourier = jnp.einsum('wn,xn->wx', table, lines, precision=high)  70.5 us
    dot_general x3, matrix products, whole_rows(): jnp.einsum('lbrjc,bjtc->lbrjt', sources, sl_weights, precision=high)  53.1 us
    div x2, local copies, waits for them, and re-layouts, local(): jnp.stack([jnp.cos(angles), -jnp.sin(angles)], axis=1)  46.4 us
  transfers between devices with their start and end apart: 15, of which 5 were waited for; matrix products, arithmetic and copies ran while one was open for 44% of the time, Pallas kernels for 6%

profile of v1, /device:TPU:0, one launch (start us, length us, event | category | flops | bytes accessed | tf_op | source)
XLA Modules:
  0.0 1747.6 jit_solution(16810908053250427617)
XLA Ops:
  6.5 20.9 %fusion.57 = (f32[1,4,640,768]{3,2,1,0:T(8,128)}, f32[4,640,768]{2,1,0:T(8,128)}, f32[4,640,768]{2,1,0:T(8,128)S(1)}, f32[4,640,768]{2,1,0:T(8,128)}, f32[1,4,640,768]{3,2,1,0:T(8,128)}, /*index=5*/f32[1,4,640,768]{3,2,1,0:T(8,128)}) fusion(f32[3,4,640,768]{3,2,1,0:T(8,128)} %param.9), kind=kLoop, calls=%fused_computation.97 | loop fusion | bytes 70778880 | tf_op jit(solution)/shard_map/slice | solution.py:79
  51.0 18.1 %fusion.59 = (f32[4,640,640]{2,1,0:T(8,128)}, f32[4,640,640]{2,1,0:T(8,128)}, f32[4,640,640]{2,1,0:T(8,128)}, f32[4,640,640]{2,1,0:T(8,128)}) fusion(f32[4,640,768]{2,1,0:T(8,128)} %get-tuple-element.18, f32[4,640,768]{2,1,0:T(8,128)} %get-tuple-element.20), kind=kLoop, calls=%fused_computation.99 | loop fusion | bytes 52428800 | tf_op jit(solution)/shard_map/slice | solution.py:84
  69.1 10.9 fusion.63
  80.0 10.1 reshape_squeeze.10
  90.1 10.1 reshape_squeeze.11
  100.2 10.1 reshape_squeeze.9
  110.6 16.0 collective-permute-start.3
  133.8 10.1 reshape.258
  151.1 10.1 reshape.259
  168.4 10.1 reshape.245
  185.8 10.1 reshape.244
  202.9 10.1 reshape.248
  220.2 10.1 reshape.249
  230.3 43.0 %select_select_fusion.2 = (f32[4,20,32,6,128]{4,3,2,1,0:T(8,128)}, f32[4,20,32,6,128]{4,3,2,1,0:T(8,128)}, f32[4,20,32,6,128]{4,3,2,1,0:T(8,128)}) fusion(f32[4,20,32,6,128]{4,3,2,1,0:T(8,128)} %reshape.244, f32[4,20,32,6,128]{4,3,2,1,0:T(8,128)} %reshape.245, f32[4,20,32,6,128]{4,3,2,1,0:T(8,128)} %reshape_squeeze.9, pred[20,6]{1,0:T(8,128)(4,1)S(1)} %copy.177, ...), kind=kLoop, calls=%fused_computation.10 | loop fusion | flops 11796480 | bytes 94372080 | tf_op jit(solution)/shard_map/jit(_where)/select_n | solution.py:85
  273.3 17.7 %fusion.40 = f32[4,20,32,6,128]{4,2,0,3,1:T(8,128)} fusion(f32[20,6,128,128]{3,2,1,0:T(8,128)} %param.10, f32[4,20,32,6,128]{4,3,2,1,0:T(8,128)} %get-tuple-element.44), kind=kOutput, calls=%fused_computation.56 | convolution fusion | flops 1509949440 | bytes 23592960 | tf_op jit(solution)/shard_map/lbrjc,bjtc->lbrjt/dot_general | solution.py:86
  291.0 15.0 copy.184
  306.0 10.8 reshape.250
  329.6 17.7 %fusion.35 = f32[4,20,32,6,128]{4,2,0,3,1:T(8,128)} fusion(f32[20,6,128,128]{3,2,1,0:T(8,128)} %param.10, f32[4,20,32,6,128]{4,3,2,1,0:T(8,128)} %get-tuple-element.43), kind=kOutput, calls=%fused_computation.55 | convolution fusion | flops 1509949440 | bytes 23592960 | tf_op jit(solution)/shard_map/lbrjc,bjtc->lbrjt/dot_general | solution.py:86
  347.3 15.3 copy.179
  362.5 10.8 reshape.246
  380.4 115.0 %all-to-all-done.2 = f32[4,4,160,768]{3,2,1,0:T(8,128)} async-done(((f32[4,4,160,768]{3,2,1,0:T(8,128)}), f32[4,4,160,768]{3,2,1,0:T(8,128)}, u32[]{:S(2)}, u32[]{:S(2)}) %all-to-all-start.2) | async-done | bytes 7864352 | tf_op jit(solution)/shard_map/all_to_all | solution.py:88
  511.2 161.1 %all-to-all-done = f32[4,4,160,768]{3,2,1,0:T(8,128)} async-done(((f32[4,4,160,768]{3,2,1,0:T(8,128)}), f32[4,4,160,768]{3,2,1,0:T(8,128)}, u32[]{:S(2)}, u32[]{:S(2)}) %all-to-all-start) | async-done | bytes 7864352 | tf_op jit(solution)/shard_map/all_to_all | solution.py:88
  679.9 34.9 %fusion.27 = (f32[640,1,3072]{2,0,1:T(8,128)}, f32[640,1,3072]{2,0,1:T(8,128)}) fusion(s32[640]{0:T(1024)S(1)} %copy-done.6), kind=kLoop, calls=%fused_computation.42 | loop fusion | flops 19660800 | bytes 15731200 | tf_op jit(solution)/shard_map/cos | solution.py:130
  714.8 14.5 maximum_multiply_fusion
  729.3 27.1 %copy.175 = f32[640,2,3072]{2,1,0:T(2,128)} copy(f32[640,2,3072]{2,0,1:T(8,128)} %maximum_multiply_fusion) | data formatting | bytes 31457280 | tf_op jit(solution)/shard_map/div | solution.py:130
  756.3 19.4 %div.16 = f32[2,4,160,3072]{3,2,1,0:T(8,128)} reshape(f32[640,2,3072]{2,1,0:T(2,128)} %copy.175) | data formatting | bytes 31457280 | tf_op jit(solution)/shard_map/div | solution.py:130
  775.7 11.5 copy.205
  787.2 10.6 reshape.285
  797.9 23.4 %fusion.10 = f32[2,4,160,640]{3,2,1,0:T(8,128)S(1)} fusion(f32[2,4,160,3072]{3,2,1,0:T(8,128)} %div.16, f32[640,3072,1,1]{1,0,2,3:T(8,128)} %reshape.285), kind=kOutput, calls=%fused_computation.23 | convolution fusion | flops 15099494400 | bytes 26869760 | tf_op jit(solution)/shard_map/wn,xn->wx/dot_general | solution.py:137
  821.3 39.6 %all_to_all.50 = f32[2,4,160,640]{3,2,1,0:T(8,128)S(1)} all-to-all(f32[2,4,160,640]{3,2,1,0:T(8,128)S(1)} %fusion.10), channel_id=1, replica_groups=mesh['lat'=2,'lon'=4,'lev'=4] {'lat'}, dimensions={0} | all-to-all | bytes 6553600 | tf_op jit(solution)/shard_map/all_to_all | solution.py:139
  867.0 17.7 %fusion.45 = f32[4,20,32,6,128]{4,2,0,3,1:T(8,128)} fusion(f32[20,6,128,128]{3,2,1,0:T(8,128)} %param.10, f32[4,20,32,6,128]{4,3,2,1,0:T(8,128)} %get-tuple-element.45), kind=kOutput, calls=%fused_computation.57 | convolution fusion | flops 1509949440 | bytes 23592960 | tf_op jit(solution)/shard_map/lbrjc,bjtc->lbrjt/dot_general | solution.py:86
  884.7 15.0 copy.199
  899.6 10.8 reshape.260
  917.6 21.0 %all-to-all-done.9 = f32[2,4,160,640]{3,2,0,1:T(8,128)S(1)} async-done(((f32[2,4,160,640]{3,2,0,1:T(8,128)}), f32[2,4,160,640]{3,2,0,1:T(8,128)S(1)}, u32[]{:S(2)}, u32[]{:S(2)}) %all-to-all-start.9) | async-done | bytes 3276832 | tf_op jit(solution)/shard_map/all_to_all | solution.py:140
  965.4 150.1 %all-to-all-done.5 = f32[4,4,160,768]{3,2,1,0:T(8,128)} async-done(((f32[4,4,160,768]{3,2,1,0:T(8,128)}), f32[4,4,160,768]{3,2,1,0:T(8,128)}, u32[]{:S(2)}, u32[]{:S(2)}) %all-to-all-start.5) | async-done | bytes 7864352 | tf_op jit(solution)/shard_map/all_to_all | solution.py:88
  1115.4 11.5 copy.201
  1126.9 10.7 reshape.284
  1137.6 23.4 %fusion.12 = f32[2,4,160,640]{3,2,1,0:T(8,128)S(1)} fusion(f32[2,4,160,3072]{3,2,1,0:T(8,128)} %div.16, f32[640,3072,1,1]{1,0,2,3:T(8,128)} %reshape.284), kind=kOutput, calls=%fused_computation.25 | convolution fusion | flops 15099494400 | bytes 26869760 | tf_op jit(solution)/shard_map/wn,xn->wx/dot_general | solution.py:137
  1161.0 39.6 %all_to_all.51 = f32[2,4,160,640]{3,2,1,0:T(8,128)S(1)} all-to-all(f32[2,4,160,640]{3,2,1,0:T(8,128)S(1)} %fusion.12), channel_id=1, replica_groups=mesh['lat'=2,'lon'=4,'lev'=4] {'lat'}, dimensions={0} | all-to-all | bytes 6553600 | tf_op jit(solution)/shard_map/all_to_all | solution.py:139
  1200.9 75.0 %all_to_all.52 = f32[2,4,160,640]{3,2,0,1:T(8,128)S(1)} all-to-all(f32[2,4,160,640]{3,2,0,1:T(8,128)S(1)} %copy.202), channel_id=1, replica_groups=mesh['lat'=2,'lon'=4,'lev'=4] {'lon'}, dimensions={1} | all-to-all | bytes 6553600 | tf_op jit(solution)/shard_map/all_to_all | solution.py:140
  1312.4 97.3 %shard_map.91 = f32[1280,768]{1,0:T(8,128)} custom-call(f32[9,32]{1,0:T(8,128)} %stack.78.coef, f32[1280,768]{1,0:T(8,128)} %bitcast.137, f32[1280,768]{1,0:T(8,128)} %bitcast.136, f32[1280,768]{1,0:T(8,128)} %bitcast.138, f32[1280,768]{1,0:T(8,128)} %bitcast.139), custom_call_target="tpu_custom_call" | custom-call | flops 629145600 | bytes 19660800 | tf_op jit(solution)/shard_map/pallas_call | solution.py:49
  1424.8 10.5 reshape.282
  1435.2 23.6 %fusion.14 = f32[2,4,160,640]{3,2,1,0:T(8,128)S(1)} fusion(f32[2,4,160,3072]{3,2,1,0:T(8,128)} %div.16, f32[640,3072,1,1]{1,0,2,3:T(8,128)} %reshape.282), kind=kOutput, calls=%fused_computation.27 | convolution fusion | flops 15099494400 | bytes 26869760 | tf_op jit(solution)/shard_map/wn,xn->wx/dot_general | solution.py:137
  1458.9 39.1 %all_to_all.53 = f32[2,4,160,640]{3,2,1,0:T(8,128)S(1)} all-to-all(f32[2,4,160,640]{3,2,1,0:T(8,128)S(1)} %fusion.14), channel_id=1, replica_groups=mesh['lat'=2,'lon'=4,'lev'=4] {'lat'}, dimensions={0} | all-to-all | bytes 6553600 | tf_op jit(solution)/shard_map/all_to_all | solution.py:139
  1498.2 74.3 %all_to_all.54 = f32[2,4,160,640]{3,2,0,1:T(8,128)S(1)} all-to-all(f32[2,4,160,640]{3,2,0,1:T(8,128)S(1)} %copy.195), channel_id=1, replica_groups=mesh['lat'=2,'lon'=4,'lev'=4] {'lon'}, dimensions={1} | all-to-all | bytes 6553600 | tf_op jit(solution)/shard_map/all_to_all | solution.py:140
  1591.1 38.4 %fusion = f32[80,4,8,160]{3,2,1,0:T(8,128)S(1)} fusion(f32[4,80,8,1280]{3,2,0,1:T(8,128)} %all-gather.10.cloned.1.call-done, f32[80,160,1280]{2,1,0:T(8,128)} %param.17), kind=kOutput, calls=%fused_computation | convolution fusion | flops 3145728000 | bytes 80281600 | tf_op jit(solution)/shard_map/Lmxs,mns->mLxn/dot_general | solution.py:144
  1631.4 36.6 %fusion.2 = f32[80,4,8,160]{3,2,1,0:T(8,128)S(1)} fusion(f32[4,80,8,1280]{3,2,0,1:T(8,128)} %all-gather.8.cloned.1.call-done, f32[80,160,1280]{2,1,0:T(8,128)} %param.17), kind=kOutput, calls=%fused_computation.2 | convolution fusion | flops 3145728000 | bytes 80281600 | tf_op jit(solution)/shard_map/Lmxs,mns->mLxn/dot_general | solution.py:144
  1674.2 36.1 %fusion.4 = f32[80,4,8,160]{3,2,1,0:T(8,128)S(1)} fusion(f32[4,80,8,1280]{3,2,0,1:T(8,128)} %all-gather.6.cloned.1.call-done, f32[80,160,1280]{2,1,0:T(8,128)} %param.17), kind=kOutput, calls=%fused_computation.4 | convolution fusion | flops 3145728000 | bytes 80281600 | tf_op jit(solution)/shard_map/Lmxs,mns->mLxn/dot_general | solution.py:144
  (124 shorter events, 258.9 us)
Async XLA Ops:
  27.4 17.1 copy-start
  27.4 17.1 copy-start.5
  32.9 77.7 %collective-permute-start.4 = (f32[4,640,128]{2,1,0:T(8,128)}, f32[4,640,128]{2,1,0:T(8,128)}, u32[]{:S(2)}, u32[]{:S(2)}) collective-permute-start(f32[4,640,128]{2,1,0:T(8,128)} %get-tuple-element.32), channel_id=1, source_target_pairs={{0,4},{4,8},{8,12},{12,0},{1,5},{5,9},{9,13},{13,1},{2,6},{6,10},{... | collective-permute-start | bytes 3932168 | tf_op jit(solution)/shard_map/ppermute | solution.py:80
  35.9 108.1 %collective-permute-start.5 = (f32[4,640,128]{2,1,0:T(8,128)}, f32[4,640,128]{2,1,0:T(8,128)}, u32[]{:S(2)}, u32[]{:S(2)}) collective-permute-start(f32[4,640,128]{2,1,0:T(8,128)} %get-tuple-element.31), channel_id=1, source_target_pairs={{4,0},{8,4},{12,8},{0,12},{5,1},{9,5},{13,9},{1,13},{6,2},{10,6},{... | collective-permute-start | bytes 3932168 | tf_op jit(solution)/shard_map/ppermute | solution.py:81
  41.3 120.0 %collective-permute-start.1 = (f32[4,640,128]{2,1,0:T(8,128)}, f32[4,640,128]{2,1,0:T(8,128)}, u32[]{:S(2)}, u32[]{:S(2)}) collective-permute-start(f32[4,640,128]{2,1,0:T(8,128)} %get-tuple-element.27), channel_id=1, source_target_pairs={{4,0},{8,4},{12,8},{0,12},{5,1},{9,5},{13,9},{1,13},{6,2},{10,6},{... | collective-permute-start | bytes 3932168 | tf_op jit(solution)/shard_map/ppermute | solution.py:81
  43.3 135.2 %collective-permute-start = (f32[4,640,128]{2,1,0:T(8,128)}, f32[4,640,128]{2,1,0:T(8,128)}, u32[]{:S(2)}, u32[]{:S(2)}) collective-permute-start(f32[4,640,128]{2,1,0:T(8,128)} %get-tuple-element.28), channel_id=1, source_target_pairs={{0,4},{4,8},{8,12},{12,0},{1,5},{5,9},{9,13},{13,1},{2,6},{6,10},{... | collective-permute-start | bytes 3932168 | tf_op jit(solution)/shard_map/ppermute | solution.py:80
  44.6 151.4 %collective-permute-start.2 = (f32[4,640,128]{2,1,0:T(8,128)}, f32[4,640,128]{2,1,0:T(8,128)S(1)}, u32[]{:S(2)}, u32[]{:S(2)}) collective-permute-start(f32[4,640,128]{2,1,0:T(8,128)} %get-tuple-element.36), channel_id=1, source_target_pairs={{0,4},{4,8},{8,12},{12,0},{1,5},{5,9},{9,13},{13,1},{2,6},{6,10},{... | collective-permute-start | bytes 3932168 | tf_op jit(solution)/shard_map/ppermute | solution.py:80
  45.4 278.6 %all-to-all-start.1 = ((f32[4,1,960]{2,1,0:T(1,128)}), f32[4,1,960]{2,1,0:T(1,128)}, u32[]{:S(2)}, u32[]{:S(2)}) async-start(f32[4,1,960]{2,1,0:T(1,128)} %reshape.289), calls=%async_computation.1 | async-start | bytes 32768 | tf_op jit(solution)/shard_map/all_to_all | solution.py:95
  69.1 10.9 copy-start.7
  110.6 102.4 %collective-permute-start.3 = (f32[4,640,128]{2,1,0:T(8,128)S(1)}, f32[4,640,128]{2,1,0:T(8,128)}, u32[]{:S(2)}, u32[]{:S(2)}) collective-permute-start(f32[4,640,128]{2,1,0:T(8,128)S(1)} %get-tuple-element.35), channel_id=1, source_target_pairs={{4,0},{8,4},{12,8},{0,12},{5,1},{9,5},{13,9},{1,13},{6,2},{10,6},{... | collective-permute-start | bytes 3932168 | tf_op jit(solution)/shard_map/ppermute | solution.py:81
  324.0 171.4 %all-to-all-start.2 = ((f32[4,4,160,768]{3,2,1,0:T(8,128)}), f32[4,4,160,768]{3,2,1,0:T(8,128)}, u32[]{:S(2)}, u32[]{:S(2)}) async-start(f32[4,4,160,768]{3,2,1,0:T(8,128)} %copy.185), calls=%async_computation.2 | async-start | bytes 15728640 | tf_op jit(solution)/shard_map/all_to_all | solution.py:88
  495.4 176.9 %all-to-all-start = ((f32[4,4,160,768]{3,2,1,0:T(8,128)}), f32[4,4,160,768]{3,2,1,0:T(8,128)}, u32[]{:S(2)}, u32[]{:S(2)}) async-start(f32[4,4,160,768]{3,2,1,0:T(8,128)} %copy.180), calls=%async_computation | async-start | bytes 15728640 | tf_op jit(solution)/shard_map/all_to_all | solution.py:88
  501.0 799.1 %all-gather.12.cloned.1.call-start = ((), (), s32[]{:S(2)}) async-start(), calls=%async_computation.13 | async-start | bytes 9830400 | tf_op jit(solution)/shard_map/all_gather | solution.py:107
  503.8 4.5 copy-start.3
  511.2 168.7 %copy-start.6 = (s32[640]{0:T(1024)S(1)}, s32[640]{0:T(1024)}, u32[]{:S(2)}) copy-start(s32[640]{0:T(1024)} %param.16) | copy-start | bytes 7684
  862.8 75.7 %all-to-all-start.9 = ((f32[2,4,160,640]{3,2,0,1:T(8,128)}), f32[2,4,160,640]{3,2,0,1:T(8,128)S(1)}, u32[]{:S(2)}, u32[]{:S(2)}) async-start(f32[2,4,160,640]{3,2,0,1:T(8,128)} %copy.206), calls=%async_computation.9 | async-start | bytes 6553600 | tf_op jit(solution)/shard_map/all_to_all | solution.py:140
  938.6 176.9 %all-to-all-start.5 = ((f32[4,4,160,768]{3,2,1,0:T(8,128)}), f32[4,4,160,768]{3,2,1,0:T(8,128)}, u32[]{:S(2)}, u32[]{:S(2)}) async-start(f32[4,4,160,768]{3,2,1,0:T(8,128)} %copy.200), calls=%async_computation.5 | async-start | bytes 15728640 | tf_op jit(solution)/shard_map/all_to_all | solution.py:88
  944.1 647.0 %all-gather.10.cloned.1.call-start = ((), (), s32[]{:S(2)}) async-start(), calls=%async_computation.12 | async-start | bytes 16384000 | tf_op jit(solution)/shard_map/all_gather | solution.py:143
  965.3 666.1 %all-gather.8.cloned.1.call-start = ((), (), s32[]{:S(2)}) async-start(), calls=%async_computation.11 | async-start | bytes 16384000 | tf_op jit(solution)/shard_map/all_gather | solution.py:143
  1287.6 6.0 copy-start.8
  1287.6 6.0 copy-start.9
  1287.6 6.0 copy-start.10
  1293.5 380.7 %all-gather.6.cloned.1.call-start = ((), (), s32[]{:S(2)}) async-start(), calls=%async_computation.10 | async-start | bytes 16384000 | tf_op jit(solution)/shard_map/all_gather | solution.py:143
  1300.1 5.7 copy-start.1
  1306.2 3.7 copy-start.2
  1312.4 97.3 %copy-start.4 = (f32[2,160,768]{2,1,0:T(8,128)S(1)}, f32[2,160,768]{2,1,0:T(8,128)}, u32[]{:S(2)}) copy-start(f32[2,160,768]{2,1,0:T(8,128)} %copy-done.3) | copy-start | bytes 2949124
Sparse Core Ops, SparseCore 0:
  680.0 54.4 all-gather.11
  965.4 85.5 all-gather.9
  1293.6 83.2 all-gather.7
  1590.3 83.8 all-gather.5
